TPU v7x, 32 devices: a whole 2x2x4 slice. The times are simulated.
32 devices in a mesh: seq: 4 (over y, x), tensor: 8 (over z, core).
Axes of the slice: x: 2, y: 2, z: 4, core: 2. Of those that a mesh axis runs over, the one named last changes fastest.
Arguments:
- tokens: bfloat16 [4096, 4096], P(('seq', 'tensor')), may hold values from -36 to 36
- norm_gain: float32 [4096], replicated, may hold values from 0.1 to 1.9
- in_weight: bfloat16 [4096, 3, 4096], P(None, None, 'tensor'), may hold values from -0.09375 to 0.09375
- short_filter: float32 [3, 3, 4096], P(None, None, 'tensor'), may hold values from -3 to 3
- filter_spectrum: float32 [2, 8, 4096, 1024], P(None, 'seq', 'tensor'), may hold values from -4 to 4
- out_weight: bfloat16 [4096, 4096], P('tensor'), may hold values from -0.09375 to 0.09375
Outputs:
- mixer_out: bfloat16 [4096, 4096], P(('seq', 'tensor'))
All inputs are finite; a program needn't handle non-finite values.
Results may differ from a plain program's by a relative error of at most 0.012.
Values may be sent and summed in bfloat16 or wider, within the bound.
A program may use at most 192 MiB of HBM per device.

v0:
```python
import math
import jax
import jax.numpy as jnp
from jax import lax
from jax.sharding import PartitionSpec as P

MONARCH = 32
TAPS = 3
EPS = 1e-06
TABLE_PRECISION = lax.Precision.HIGH
FULL_TURN = 2.0 * math.pi


def shifted(block, axis, distance):
    devices = range(lax.axis_size(axis))
    route = [(i - distance, i) for i in devices if i - distance in devices]
    return lax.ppermute(block, axis, route)


def as_sent(value):
    return jax.tree.map(lambda a: a.astype(jnp.bfloat16) if a.dtype == jnp.float32 else a, value)


def turn_table(count, orient):
    index = jnp.arange(count, dtype=jnp.int32)
    angle = FULL_TURN * (index[:, None] * index[None, :] % count).astype(jnp.float32) / count
    return (jnp.cos(angle), orient * jnp.sin(angle))


def twist(real_part, imag_part, table_cos, table_sin, form):
    cos_real = jnp.einsum(form, table_cos, real_part, precision=TABLE_PRECISION)
    sin_real = jnp.einsum(form, table_sin, real_part, precision=TABLE_PRECISION)
    cos_imag = jnp.einsum(form, table_cos, imag_part, precision=TABLE_PRECISION)
    sin_imag = jnp.einsum(form, table_sin, imag_part, precision=TABLE_PRECISION)
    return (cos_real - sin_imag, cos_imag + sin_real)


def local_dft(real_part, imag_part, orient):
    length = real_part.shape[-1]
    first = MONARCH
    second = length // first
    leading = real_part.shape[:-1]
    real_part = real_part.reshape(leading + (first, second))
    imag_part = imag_part.reshape(leading + (first, second))
    cos_first, sin_first = turn_table(first, orient)
    real_part, imag_part = twist(real_part, imag_part, cos_first, sin_first, "ca,...ab->...cb")
    outer_index = jnp.arange(first, dtype=jnp.int32)[:, None]
    inner_index = jnp.arange(second, dtype=jnp.int32)[None, :]
    angle = FULL_TURN * (outer_index * inner_index % length).astype(jnp.float32) / length
    cos_middle = jnp.cos(angle)
    sin_middle = orient * jnp.sin(angle)
    real_part, imag_part = (
        real_part * cos_middle - imag_part * sin_middle,
        imag_part * cos_middle + real_part * sin_middle,
    )
    cos_second, sin_second = turn_table(second, orient)
    real_part, imag_part = twist(real_part, imag_part, cos_second, sin_second, "db,...cb->...dc")
    return (real_part.reshape(leading + (length,)), imag_part.reshape(leading + (length,)))


def rotate(real_part, imag_part, freq_index, row_index, total_length, orient):
    angle = (
        FULL_TURN
        * (freq_index[:, None] * row_index[None, :] % total_length).astype(jnp.float32)
        / total_length
    )
    cos_turn = jnp.cos(angle)[:, None, :]
    sin_turn = orient * jnp.sin(angle)[:, None, :]
    return (
        real_part * cos_turn - imag_part * sin_turn,
        imag_part * cos_turn + real_part * sin_turn,
    )


def block_dft(blocks, row_index, total_length):
    count = blocks.shape[0]
    freq_count = 2 * count
    freq_index = jnp.arange(freq_count, dtype=jnp.int32)
    block_index = jnp.arange(count, dtype=jnp.int32)
    angle = (
        FULL_TURN
        * (freq_index[:, None] * block_index[None, :] % freq_count).astype(jnp.float32)
        / freq_count
    )
    real_part = jnp.einsum("ks,scr->kcr", jnp.cos(angle), blocks, precision=TABLE_PRECISION)
    imag_part = -jnp.einsum("ks,scr->kcr", jnp.sin(angle), blocks, precision=TABLE_PRECISION)
    real_part, imag_part = rotate(real_part, imag_part, freq_index, row_index, total_length, -1.0)
    return jnp.stack([real_part, imag_part])


def block_idft(real_part, imag_part, total_length):
    freq_count = real_part.shape[0]
    count = freq_count // 2
    block_index = jnp.arange(count, dtype=jnp.int32)
    freq_index = jnp.arange(freq_count, dtype=jnp.int32)
    angle = (
        FULL_TURN
        * (block_index[:, None] * freq_index[None, :] % freq_count).astype(jnp.float32)
        / freq_count
    )
    value = jnp.einsum("sk,kcr->scr", jnp.cos(angle), real_part, precision=TABLE_PRECISION)
    value = value - jnp.einsum("sk,kcr->scr", jnp.sin(angle), imag_part, precision=TABLE_PRECISION)
    return value / total_length


def apply_filter(frequency, filter_part):
    real_part, imag_part = local_dft(frequency[0], frequency[1], -1.0)
    filter_real = filter_part[0]
    filter_imag = filter_part[1]
    product_real = real_part * filter_real - imag_part * filter_imag
    product_imag = real_part * filter_imag + imag_part * filter_real
    return local_dft(product_real, product_imag, 1.0)


def per_device(tokens, norm_gain, in_weight, short_filter, filter_spectrum, out_weight):
    seq_count = lax.axis_size("seq")
    seq_place = lax.axis_index("seq")
    inputs = tokens.astype(jnp.float32)
    square_mean = jnp.mean(inputs * inputs, axis=-1, keepdims=True)
    normed = (inputs / jnp.sqrt(square_mean + EPS) * norm_gain).astype(jnp.bfloat16)
    model_width = in_weight.shape[0]
    width = in_weight.shape[2]
    flat_weight = in_weight.reshape(model_width, 3 * width)
    projected = jnp.dot(
        lax.all_gather(normed, "tensor", axis=0, tiled=True),
        flat_weight,
        preferred_element_type=jnp.float32,
    ).astype(jnp.bfloat16)
    rows = projected.shape[0]
    carried = shifted(projected[rows - (TAPS - 1) :], "seq", 1)
    extended = (
        jnp.concatenate([carried, projected], axis=0)
        .astype(jnp.float32)
        .reshape(rows + TAPS - 1, 3, width)
    )
    short = jnp.zeros((rows, 3, width), jnp.float32)
    for offset in range(TAPS):
        short = (
            short + short_filter[offset] * extended[TAPS - 1 - offset : TAPS - 1 - offset + rows]
        )
    queries = short[:, 0]
    product_cols = (short[:, 1] * short[:, 2]).astype(jnp.bfloat16).T
    total_length = 2 * rows * seq_count
    all_rows = jnp.arange(rows, dtype=jnp.int32)
    piece_rows = rows // seq_count
    gathered = lax.all_to_all(
        product_cols.reshape(1, width, rows), "seq", split_axis=2, concat_axis=0, tiled=True
    )
    own_rows = seq_place * piece_rows + jnp.arange(piece_rows, dtype=jnp.int32)
    partial_spec = block_dft(gathered.astype(jnp.float32), own_rows, total_length)
    frequency = lax.all_to_all(
        partial_spec.astype(jnp.bfloat16), "seq", split_axis=1, concat_axis=3, tiled=True
    ).astype(partial_spec.dtype)
    real_part, imag_part = apply_filter(frequency, filter_spectrum)
    own_freq = 2 * seq_place + jnp.arange(2, dtype=jnp.int32)
    real_part, imag_part = rotate(real_part, imag_part, own_freq, all_rows, total_length, 1.0)
    returned = lax.all_to_all(
        jnp.stack([real_part, imag_part]).astype(jnp.bfloat16),
        "seq",
        split_axis=3,
        concat_axis=1,
        tiled=True,
    ).astype(jnp.float32)
    value_blocks = block_idft(returned[0], returned[1], total_length)
    value_cols = lax.all_to_all(
        as_sent(value_blocks), "seq", split_axis=0, concat_axis=2, tiled=True
    ).astype(value_blocks.dtype)
    long_conv = value_cols[0].T
    gated = (queries * long_conv).astype(jnp.bfloat16)
    summed = lax.psum_scatter(
        jnp.dot(gated, out_weight, preferred_element_type=jnp.float32).astype(jnp.bfloat16),
        "tensor",
        scatter_dimension=0,
        tiled=True,
    ).astype(jnp.float32)
    return (inputs + summed).astype(jnp.bfloat16)


def solution(mesh):
    in_specs = (
        P(("seq", "tensor"), None),
        P(),
        P(None, None, "tensor"),
        P(None, None, "tensor"),
        P(None, "seq", "tensor", None),
        P("tensor", None),
    )
    out_specs = P(("seq", "tensor"), None)
    return jax.shard_map(
        per_device, mesh=mesh, in_specs=in_specs, out_specs=out_specs, check_vma=False
    )
```

profile of v0, /device:TPU:0, one launch (start us, length us, event | category | flops | bytes accessed | tf_op | source)
XLA Modules:
  0.0 549.9 jit_solution(9565816952888031319)
XLA Ops:
  10.6 17.1 %copy.89 = bf16[4096,3,512]{0,2,1:T(8,128)(2,1)} copy(bf16[4096,3,512]{2,0,1:T(8,128)(2,1)} %param.8) | data formatting | bytes 25165824 | tf_op args[2]
  27.7 67.8 %all-gather.2.cloned.1.call-done = bf16[1024,4096]{1,0:T(8,128)(2,1)} async-done(((bf16[128,4096]{1,0:T(8,128)(2,1)}), bf16[1024,4096]{1,0:T(8,128)(2,1)}) %all-gather.2.cloned.1.call-update) | async-done | bytes 8388624 | tf_op jit(solution)/shard_map/all_gather | solution.py:125
  95.5 18.3 %convolution_convert_fusion.1 = bf16[1024,1536]{1,0:T(8,128)(2,1)S(1)} fusion(bf16[1024,4096]{1,0:T(8,128)(2,1)} %all-gather.2.cloned.1.call-done, bf16[4096,1536]{0,1:T(8,128)(2,1)} %bitcast.210), kind=kOutput, calls=%fused_computation.50 | convolution fusion | flops 12886474752 | bytes 24117248 | tf_op jit(solution)/shard_map/dot_general | solution.py:124
  119.5 7.4 %fusion.229 = (f32[1024,1536]{1,0:T(8,128)}, f32[1024,1536]{1,0:T(8,128)}, f32[1024,1536]{1,0:T(8,128)}) fusion(f32[1026,1536]{1,0:T(8,128)S(1)} %maximum_convert_fusion), kind=kLoop, calls=%fused_computation.263 | loop fusion | bytes 37748736 | tf_op jit(solution)/shard_map/slice | solution.py:139
  127.0 6.6 %copy.90 = f32[1024,1536]{0,1:T(8,128)} copy(f32[1024,1536]{1,0:T(8,128)} %get-tuple-element.17) | data formatting | bytes 12582912 | tf_op jit(solution)/shard_map/slice | solution.py:139
  133.5 6.6 %copy.91 = f32[1024,1536]{0,1:T(8,128)} copy(f32[1024,1536]{1,0:T(8,128)} %get-tuple-element.19) | data formatting | bytes 12582912 | tf_op jit(solution)/shard_map/slice | solution.py:139
  140.1 6.6 %copy.92 = f32[1024,1536]{0,1:T(8,128)} copy(f32[1024,1536]{1,0:T(8,128)} %get-tuple-element.18) | data formatting | bytes 12582912 | tf_op jit(solution)/shard_map/slice | solution.py:139
  146.7 7.1 %multiply_add_fusion = f32[1024,3,512]{0,2,1:T(8,128)S(1)} fusion(f32[1024,3,512]{0,2,1:T(8,128)} %bitcast.203, f32[1024,3,512]{0,2,1:T(8,128)} %bitcast.202, f32[1024,3,512]{0,2,1:T(8,128)} %bitcast.201, f32[3,512]{1,0:T(4,128)S(1)} %get-tuple-element.25, f32[3,512]{1,0:T(4,128)S(1)} %get-tuple-element.26, f32[3,512]{1,0:T(4,128)S(1)} %get-tuple-element.24), kind=kLoop, calls=%fused_computation.1 | loop fusion | flops 7864320 | bytes 25184256 | tf_op jit(solution)/shard_map/add | solution.py:139
  159.5 7.0 %reduce = bf16[1024,512]{1,0:T(8,128)(2,1)S(1)} reduce(bf16[1024,1,512]{2,1,0:T(2,128)(2,1)S(1)} %bitcast.212, bf16[]{:T(256)} %broadcast.422), dimensions={1}, to_apply=%bitcast.198.reduce_sub_computation | reduce | bytes 2097154
  173.3 13.5 %all-to-all-done = bf16[4,2,65536]{2,1,0:T(2,128)(2,1)S(1)} async-done(((bf16[4,2,65536]{2,1,0:T(2,128)(2,1)}), bf16[4,2,65536]{2,1,0:T(2,128)(2,1)S(1)}, u32[]{:S(2)}, u32[]{:S(2)}) %all-to-all-start) | async-done | bytes 1048608 | tf_op jit(solution)/shard_map/all_to_all | solution.py:146
  201.9 8.5 %fusion.228 = (f32[1,2,512,1024]{3,2,1,0:T(8,128)}, f32[1,2,512,1024]{3,2,1,0:T(8,128)}) fusion(f32[2,2,512,1024]{3,2,1,0:T(8,128)} %param.10), kind=kLoop, calls=%fused_computation.262 | loop fusion | bytes 16777216 | tf_op jit(solution)/shard_map/slice | solution.py:108
  210.4 5.4 copy.134
  215.8 5.4 copy.135
  221.6 27.7 %all-to-all-done.1 = bf16[2,8,512,256]{3,2,0,1:T(8,128)(2,1)} async-done(((bf16[2,8,512,256]{3,2,0,1:T(8,128)(2,1)}), bf16[2,8,512,256]{3,2,0,1:T(8,128)(2,1)}, u32[]{:S(2)}, u32[]{:S(2)}) %all-to-all-start.1) | async-done | bytes 4194336 | tf_op jit(solution)/shard_map/all_to_all | solution.py:151
  281.1 6.7 %fusion.18 = f32[2,512,32,32]{1,3,2,0:T(8,128)} fusion(f32[2,512,32,32]{1,2,3,0:T(8,128)S(1)} %get-tuple-element.10), kind=kOutput, calls=%fused_computation.42 | convolution fusion | flops 201340928 | bytes 8388608 | tf_op jit(solution)/shard_map/db,...cb->...dc/dot_general | solution.py:33
  287.7 5.1 fusion.26
  292.8 11.7 %fusion.6 = (f32[2,512,32,32]{1,2,3,0:T(8,128)S(1)}, f32[2,512,32,32]{1,2,3,0:T(8,128)S(1)}) fusion(f32[2,512,32,32]{1,3,2,0:T(8,128)S(1)} %fusion.26, f32[2,512,32,32]{1,3,2,0:T(8,128)} %bitcast.207, f32[2,512,32,32]{1,3,2,0:T(8,128)S(1)} %bitcast.206, f32[2,512,32,32]{1,3,2,0:T(8,128)} %fusion.18, f32[2,512,32,32]{1,2,3,0:T(8,128)S(1)} %get-tuple-element.9), kind=kOutput, calls=%fused_computation.20 | convolution fusion | flops 208681984 | bytes 29360128 | tf_op jit(solution)/shard_map/db,...cb->...dc/dot_general | solution.py:32
  325.5 5.1 subtract_bitcast_fusion
  343.3 6.3 %copy.123 = bf16[2,2,512,1024]{2,1,0,3:T(2,128)(2,1)} copy(bf16[2,2,512,1024]{2,3,1,0:T(8,128)(2,1)S(1)} %pad_maximum_fusion.1) | data formatting | bytes 8388608 | tf_op jit(solution)/shard_map/stack | solution.py:158
  349.6 51.2 %all_to_all.57 = bf16[2,2,512,1024]{2,1,0,3:T(2,128)(2,1)S(1)} all-to-all(bf16[2,2,512,1024]{2,1,0,3:T(2,128)(2,1)} %copy.123), channel_id=1, replica_groups=mesh['seq'=4,'tensor'=8] {'seq'}, dimensions={3} | all-to-all | bytes 8388608 | tf_op jit(solution)/shard_map/all_to_all | solution.py:157
  414.1 6.3 %copy.126 = bf16[1,4,2,512,256]{4,2,1,3,0:T(2,128)(2,1)} copy(bf16[1,4,2,512,256]{3,4,1,2,0:T(8,128)(2,1)} %get-tuple-element.20) | data formatting | bytes 4194304 | tf_op jit(solution)/shard_map/slice | solution.py:164
  427.8 14.8 %all_to_all.58 = bf16[4,512,256]{2,1,0:T(8,128)(2,1)S(1)} all-to-all(bf16[4,512,256]{2,1,0:T(8,128)(2,1)S(1)} %copy.127), channel_id=1, replica_groups=mesh['seq'=4,'tensor'=8] {'seq'}, dimensions={0} | all-to-all | bytes 2097152 | tf_op jit(solution)/shard_map/all_to_all | solution.py:165
  445.0 8.6 %convolution_convert_fusion = bf16[1024,4096]{1,0:T(8,128)(2,1)} fusion(bf16[512,4096]{1,0:T(8,128)(2,1)S(1)} %copy-done.6, f32[1024,3,512]{0,2,1:T(8,128)} %copy-done.1, f32[512,1024]{1,0:T(8,128)S(1)} %bitcast.216), kind=kOutput, calls=%fused_computation | convolution fusion | flops 4300210176 | bytes 16777216 | tf_op jit(solution)/shard_map/dot_general | solution.py:171
  453.7 86.8 %reduce-scatter.2.cloned.1.call-done = bf16[128,4096]{1,0:T(8,128)(2,1)} async-done(((bf16[1024,4096]{1,0:T(8,128)(2,1)}), bf16[128,4096]{1,0:T(8,128)(2,1)}) %reduce-scatter.2.cloned.1.call-update) | async-done | bytes 1048592 | tf_op jit(solution)/shard_map/reduce_scatter | solution.py:170
  (82 shorter events, 128.4 us)
Async XLA Ops:
  6.5 89.0 %all-gather.2.cloned.1.call-start = ((), (), s32[]{:S(2)}) async-start(), calls=%async_computation.5 | async-start | bytes 9437184 | tf_op jit(solution)/shard_map/all_gather | solution.py:125
  95.5 21.7 %copy-start.5 = (f32[3,3,512]{2,1,0:T(4,128)S(1)}, f32[3,3,512]{2,1,0:T(4,128)}, u32[]{:S(2)}) copy-start(f32[3,3,512]{2,1,0:T(4,128)} %param.9) | copy-start | bytes 55300
  113.8 4.7 collective-permute-start
  153.8 2.7 copy-start.1
  168.6 18.3 %all-to-all-start = ((bf16[4,2,65536]{2,1,0:T(2,128)(2,1)}), bf16[4,2,65536]{2,1,0:T(2,128)(2,1)S(1)}, u32[]{:S(2)}, u32[]{:S(2)}) async-start(bf16[4,2,65536]{2,1,0:T(2,128)(2,1)} %reshape.261), calls=%async_computation | async-start | bytes 2097152 | tf_op jit(solution)/shard_map/all_to_all | solution.py:146
  196.7 52.6 %all-to-all-start.1 = ((bf16[2,8,512,256]{3,2,0,1:T(8,128)(2,1)}), bf16[2,8,512,256]{3,2,0,1:T(8,128)(2,1)}, u32[]{:S(2)}, u32[]{:S(2)}) async-start(bf16[2,8,512,256]{3,2,0,1:T(8,128)(2,1)} %copy.96), calls=%async_computation.1 | async-start | bytes 8388608 | tf_op jit(solution)/shard_map/all_to_all | solution.py:151
  201.5 338.9 %reduce-scatter.2.cloned.1.call-start = ((), (), s32[]{:S(2)}) async-start(), calls=%async_computation.6 | async-start | bytes 9437184 | tf_op jit(solution)/shard_map/reduce_scatter | solution.py:170
  265.7 4.0 copy-start
  265.8 4.0 copy-start.3
  287.7 5.1 copy-start.2
  442.8 2.2 copy-start.6
  453.6 86.8 %copy-start.4 = (bf16[128,4096]{1,0:T(8,128)(2,1)S(1)}, bf16[128,4096]{1,0:T(8,128)(2,1)}, u32[]{:S(2)}) copy-start(bf16[128,4096]{1,0:T(8,128)(2,1)} %param.6) | copy-start | bytes 3145732
Sparse Core Ops, SparseCore 0:
  10.7 84.7 all-gather.1
  453.8 86.5 reduce-scatter.1
where the time goes:
time: 556 us; the launch traced here: 550 us
  waiting for transfers between devices  197 us (35%)
  local copies, waits for them, and re-layouts  123 us (22%)
  matrix products  112 us (20%)
  blocking collectives  65.9 us (12%)
  other arithmetic  25.6 us (5%)
  between operations  14.1 us (3%)
  starting transfers between devices  12.9 us (2%)
    reduce_scatter x1, waiting for transfers between devices, per_device(): lax.psum_scatter(jnp.dot(gated, out_weight, preferred_element_type=jnp.fl...  86.8 us
    all_gather x1, waiting for transfers between devices, per_device(): lax.all_gather(normed, 'tensor', axis=0, tiled=True)  67.8 us
    all_to_all x1, blocking collectives, per_device(): lax.all_to_all(jnp.stack([real_part, imag_part]).astype(jnp.bfloat16), 's...  51.2 us
    unnamed x22, local copies, waits for them, and re-layouts  35.2 us
    all_to_all x1, waiting for transfers between devices, per_device(): lax.all_to_all(partial_spec.astype(jnp.bfloat16), 'seq', split_axis=1, co...  27.7 us
    slice x4, local copies, waits for them, and re-layouts, per_device(): extended[TAPS - 1 - offset:TAPS - 1 - offset + rows]  27.1 us
    dot_general x4, matrix products, twist(): sin_real = jnp.einsum(form, table_sin, real_part, precision=TABLE_PRECISION)  24.6 us
    dot_general x1, matrix products, per_device(): jnp.dot(lax.all_gather(normed, 'tensor', axis=0, tiled=True), flat_weight...  18.3 us
  transfers between devices with their start and end apart: 5, of which 5 were waited for; matrix products, arithmetic and copies ran while one was open for 7% of the time, Pallas kernels for 0%

commit v1 on v0

--- a/solution.py
+++ b/solution.py
@@ -154,12 +154,20 @@
     real_part, imag_part = apply_filter(frequency, filter_spectrum)
     own_freq = 2 * seq_place + jnp.arange(2, dtype=jnp.int32)
     real_part, imag_part = rotate(real_part, imag_part, own_freq, all_rows, total_length, 1.0)
-    returned = lax.all_to_all(
-        jnp.stack([real_part, imag_part]).astype(jnp.bfloat16),
-        "seq",
-        split_axis=3,
-        concat_axis=1,
-        tiled=True,
+    returned = jnp.concatenate(
+        lax.all_to_all(
+            jnp.stack(
+                jnp.split(
+                    jnp.stack([real_part, imag_part]).astype(jnp.bfloat16),
+                    lax.axis_size("seq"),
+                    axis=3,
+                )
+            ),
+            "seq",
+            0,
+            0,
+        ),
+        axis=1,
     ).astype(jnp.float32)
     value_blocks = block_idft(returned[0], returned[1], total_length)
     value_cols = lax.all_to_all(

time: 556 us -> 537 us (0.966)
  local copies, waits for them, and re-layouts: 123 us -> 105 us
    slice x3 -> x1, local copies, waits for them, and re-layouts: 13.7 us -> 1.6 us  [per_device(): value_blocks = block_idft(returned[0], returned[1], total_length)]
    another operation x1 -> x0, local copies, waits for them, and re-layouts: 6.26 us -> none  [per_device(): jnp.stack([real_part, imag_part]).astype(jnp.bfloat16)]
where the time goes in v1:
time: 537 us; the launch traced here: 531 us
  waiting for transfers between devices  197 us (37%)
  matrix products  112 us (21%)
  local copies, waits for them, and re-layouts  105 us (20%)
  blocking collectives  64.8 us (12%)
  other arithmetic  25.9 us (5%)
  between operations  14.3 us (3%)
  starting transfers between devices  12.9 us (2%)
    reduce_scatter x1, waiting for transfers between devices, per_device(): lax.psum_scatter(jnp.dot(gated, out_weight, preferred_element_type=jnp.fl...  86.7 us
    all_gather x1, waiting for transfers between devices, per_device(): lax.all_gather(normed, 'tensor', axis=0, tiled=True)  67.8 us
    all_to_all x1, blocking collectives, per_device(): lax.all_to_all(jnp.stack(jnp.split(jnp.stack([real_part, imag_part]).asty...  50.2 us
    unnamed x22, local copies, waits for them, and re-layouts  35.2 us
    all_to_all x1, waiting for transfers between devices, per_device(): lax.all_to_all(partial_spec.astype(jnp.bfloat16), 'seq', split_axis=1, co...  27.7 us
    slice x4, local copies, waits for them, and re-layouts, per_device(): extended[TAPS - 1 - offset:TAPS - 1 - offset + rows]  27 us
    dot_general x4, matrix products, twist(): sin_real = jnp.einsum(form, table_sin, real_part, precision=TABLE_PRECISION)  24.6 us
    dot_general x1, matrix products, per_device(): jnp.dot(lax.all_gather(normed, 'tensor', axis=0, tiled=True), flat_weight...  18.3 us
  transfers between devices with their start and end apart: 5, of which 5 were waited for; matrix products, arithmetic and copies ran while one was open for 7% of the time, Pallas kernels for 0%

profile of v1, /device:TPU:0, one launch (start us, length us, event | category | flops | bytes accessed | tf_op | source)
XLA Modules:
  0.0 531.4 jit_solution(12565679409207022833)
XLA Ops:
  10.6 17.1 %copy.90 = bf16[4096,3,512]{0,2,1:T(8,128)(2,1)} copy(bf16[4096,3,512]{2,0,1:T(8,128)(2,1)} %param.8) | data formatting | bytes 25165824 | tf_op args[2]
  27.8 67.8 %all-gather.2.cloned.1.call-done = bf16[1024,4096]{1,0:T(8,128)(2,1)} async-done(((bf16[128,4096]{1,0:T(8,128)(2,1)}), bf16[1024,4096]{1,0:T(8,128)(2,1)}) %all-gather.2.cloned.1.call-update) | async-done | bytes 8388624 | tf_op jit(solution)/shard_map/all_gather | solution.py:125
  95.5 18.3 %convolution_convert_fusion.1 = bf16[1024,1536]{1,0:T(8,128)(2,1)S(1)} fusion(bf16[1024,4096]{1,0:T(8,128)(2,1)} %all-gather.2.cloned.1.call-done, bf16[4096,1536]{0,1:T(8,128)(2,1)} %bitcast.214), kind=kOutput, calls=%fused_computation.56 | convolution fusion | flops 12886474752 | bytes 24117248 | tf_op jit(solution)/shard_map/dot_general | solution.py:124
  119.5 7.2 %fusion.236 = (f32[1024,1536]{1,0:T(8,128)}, f32[1024,1536]{1,0:T(8,128)}, f32[1024,1536]{1,0:T(8,128)}) fusion(f32[1026,1536]{1,0:T(8,128)S(1)} %maximum_convert_fusion), kind=kLoop, calls=%fused_computation.277 | loop fusion | bytes 37748736 | tf_op jit(solution)/shard_map/slice | solution.py:139
  126.8 6.6 %copy.91 = f32[1024,1536]{0,1:T(8,128)} copy(f32[1024,1536]{1,0:T(8,128)} %get-tuple-element.17) | data formatting | bytes 12582912 | tf_op jit(solution)/shard_map/slice | solution.py:139
  133.4 6.6 %copy.92 = f32[1024,1536]{0,1:T(8,128)} copy(f32[1024,1536]{1,0:T(8,128)} %get-tuple-element.19) | data formatting | bytes 12582912 | tf_op jit(solution)/shard_map/slice | solution.py:139
  140.0 6.6 %copy.93 = f32[1024,1536]{0,1:T(8,128)} copy(f32[1024,1536]{1,0:T(8,128)} %get-tuple-element.18) | data formatting | bytes 12582912 | tf_op jit(solution)/shard_map/slice | solution.py:139
  146.6 7.1 %multiply_add_fusion = f32[1024,3,512]{0,2,1:T(8,128)S(1)} fusion(f32[1024,3,512]{0,2,1:T(8,128)} %bitcast.207, f32[1024,3,512]{0,2,1:T(8,128)} %bitcast.206, f32[1024,3,512]{0,2,1:T(8,128)} %bitcast.205, f32[3,512]{1,0:T(4,128)S(1)} %get-tuple-element.29, f32[3,512]{1,0:T(4,128)S(1)} %get-tuple-element.30, f32[3,512]{1,0:T(4,128)S(1)} %get-tuple-element.28), kind=kLoop, calls=%fused_computation.1 | loop fusion | flops 7864320 | bytes 25184256 | tf_op jit(solution)/shard_map/add | solution.py:139
  159.4 7.0 %reduce = bf16[1024,512]{1,0:T(8,128)(2,1)S(1)} reduce(bf16[1024,1,512]{2,1,0:T(2,128)(2,1)S(1)} %bitcast.216, bf16[]{:T(256)} %broadcast.422), dimensions={1}, to_apply=%bitcast.202.reduce_sub_computation | reduce | bytes 2097154
  173.2 13.5 %all-to-all-done = bf16[4,2,65536]{2,1,0:T(2,128)(2,1)S(1)} async-done(((bf16[4,2,65536]{2,1,0:T(2,128)(2,1)}), bf16[4,2,65536]{2,1,0:T(2,128)(2,1)S(1)}, u32[]{:S(2)}, u32[]{:S(2)}) %all-to-all-start) | async-done | bytes 1048608 | tf_op jit(solution)/shard_map/all_to_all | solution.py:146
  196.6 4.9 all-to-all-start.1
  201.8 8.6 %fusion.235 = (f32[1,2,512,1024]{3,2,1,0:T(8,128)}, f32[1,2,512,1024]{3,2,1,0:T(8,128)}) fusion(f32[2,2,512,1024]{3,2,1,0:T(8,128)} %param.10), kind=kLoop, calls=%fused_computation.276 | loop fusion | bytes 16777216 | tf_op jit(solution)/shard_map/slice | solution.py:108
  210.4 5.4 %copy.135 = f32[1,2,512,1024]{2,3,1,0:T(8,128)} copy(f32[1,2,512,1024]{3,2,1,0:T(8,128)} %get-tuple-element.15) | data formatting | bytes 8388608
  215.7 5.4 %copy.136 = f32[1,2,512,1024]{2,3,1,0:T(8,128)} copy(f32[1,2,512,1024]{3,2,1,0:T(8,128)} %get-tuple-element.16) | data formatting | bytes 8388608
  221.5 27.7 %all-to-all-done.1 = bf16[2,8,512,256]{3,2,0,1:T(8,128)(2,1)} async-done(((bf16[2,8,512,256]{3,2,0,1:T(8,128)(2,1)}), bf16[2,8,512,256]{3,2,0,1:T(8,128)(2,1)}, u32[]{:S(2)}, u32[]{:S(2)}) %all-to-all-start.1) | async-done | bytes 4194336 | tf_op jit(solution)/shard_map/all_to_all | solution.py:151
  281.0 6.6 %fusion.18 = f32[2,512,32,32]{1,3,2,0:T(8,128)} fusion(f32[2,512,32,32]{1,2,3,0:T(8,128)S(1)} %get-tuple-element.10), kind=kOutput, calls=%fused_computation.48 | convolution fusion | flops 201340928 | bytes 8388608 | tf_op jit(solution)/shard_map/db,...cb->...dc/dot_general | solution.py:33
  287.6 5.1 fusion.26
  292.7 11.7 %fusion.6 = (f32[2,512,32,32]{1,2,3,0:T(8,128)S(1)}, f32[2,512,32,32]{1,2,3,0:T(8,128)S(1)}) fusion(f32[2,512,32,32]{1,3,2,0:T(8,128)S(1)} %fusion.26, f32[2,512,32,32]{1,3,2,0:T(8,128)} %bitcast.211, f32[2,512,32,32]{1,3,2,0:T(8,128)S(1)} %bitcast.210, f32[2,512,32,32]{1,3,2,0:T(8,128)} %fusion.18, f32[2,512,32,32]{1,2,3,0:T(8,128)S(1)} %get-tuple-element.9), kind=kOutput, calls=%fused_computation.26 | convolution fusion | flops 208681984 | bytes 29360128 | tf_op jit(solution)/shard_map/db,...cb->...dc/dot_general | solution.py:32
  325.4 5.1 subtract_bitcast_fusion
  333.2 5.1 add_bitcast_fusion
  343.5 50.2 %all_to_all.47 = bf16[4,2,2,512,256]{3,4,2,1,0:T(8,128)(2,1)S(1)} all-to-all(bf16[4,2,2,512,256]{3,4,2,1,0:T(8,128)(2,1)S(1)} %pad_maximum_fusion.1), channel_id=1, replica_groups=mesh['seq'=4,'tensor'=8] {'seq'}, dimensions={0} | all-to-all | bytes 8388608 | tf_op jit(solution)/shard_map/all_to_all | solution.py:158
  409.1 14.6 %all_to_all.48 = bf16[4,512,256]{2,1,0:T(8,128)(2,1)S(1)} all-to-all(bf16[4,512,256]{2,1,0:T(8,128)(2,1)S(1)} %copy.126), channel_id=1, replica_groups=mesh['seq'=4,'tensor'=8] {'seq'}, dimensions={0} | all-to-all | bytes 2097152 | tf_op jit(solution)/shard_map/all_to_all | solution.py:173
  426.1 8.8 %convolution_convert_fusion = bf16[1024,4096]{1,0:T(8,128)(2,1)} fusion(bf16[512,4096]{1,0:T(8,128)(2,1)S(1)} %copy-done.6, f32[1024,3,512]{0,2,1:T(8,128)} %copy-done.1, f32[512,1024]{1,0:T(8,128)S(1)} %bitcast.222), kind=kOutput, calls=%fused_computation | convolution fusion | flops 4300210176 | bytes 16777216 | tf_op jit(solution)/shard_map/dot_general | solution.py:179
  434.9 86.7 %reduce-scatter.2.cloned.1.call-done = bf16[128,4096]{1,0:T(8,128)(2,1)} async-done(((bf16[1024,4096]{1,0:T(8,128)(2,1)}), bf16[128,4096]{1,0:T(8,128)(2,1)}) %reduce-scatter.2.cloned.1.call-update) | async-done | bytes 1048592 | tf_op jit(solution)/shard_map/reduce_scatter | solution.py:178
  (79 shorter events, 113.3 us)
Async XLA Ops:
  6.5 89.0 %all-gather.2.cloned.1.call-start = ((), (), s32[]{:S(2)}) async-start(), calls=%async_computation.5 | async-start | bytes 9437184 | tf_op jit(solution)/shard_map/all_gather | solution.py:125
  95.5 21.7 %copy-start.5 = (f32[3,3,512]{2,1,0:T(4,128)S(1)}, f32[3,3,512]{2,1,0:T(4,128)}, u32[]{:S(2)}) copy-start(f32[3,3,512]{2,1,0:T(4,128)} %param.9) | copy-start | bytes 55300
  113.8 4.8 collective-permute-start
  153.7 2.7 copy-start.1
  168.5 18.3 %all-to-all-start = ((bf16[4,2,65536]{2,1,0:T(2,128)(2,1)}), bf16[4,2,65536]{2,1,0:T(2,128)(2,1)S(1)}, u32[]{:S(2)}, u32[]{:S(2)}) async-start(bf16[4,2,65536]{2,1,0:T(2,128)(2,1)} %reshape.266), calls=%async_computation | async-start | bytes 2097152 | tf_op jit(solution)/shard_map/all_to_all | solution.py:146
  196.6 52.6 %all-to-all-start.1 = ((bf16[2,8,512,256]{3,2,0,1:T(8,128)(2,1)}), bf16[2,8,512,256]{3,2,0,1:T(8,128)(2,1)}, u32[]{:S(2)}, u32[]{:S(2)}) async-start(bf16[2,8,512,256]{3,2,0,1:T(8,128)(2,1)} %copy.97), calls=%async_computation.1 | async-start | bytes 8388608 | tf_op jit(solution)/shard_map/all_to_all | solution.py:151
  201.4 320.2 %reduce-scatter.2.cloned.1.call-start = ((), (), s32[]{:S(2)}) async-start(), calls=%async_computation.6 | async-start | bytes 9437184 | tf_op jit(solution)/shard_map/reduce_scatter | solution.py:178
  265.6 4.0 copy-start
  265.6 4.0 copy-start.3
  287.6 5.1 copy-start.2
  423.9 2.2 copy-start.6
  434.9 86.8 %copy-start.4 = (bf16[128,4096]{1,0:T(8,128)(2,1)S(1)}, bf16[128,4096]{1,0:T(8,128)(2,1)}, u32[]{:S(2)}) copy-start(bf16[128,4096]{1,0:T(8,128)(2,1)} %param.6) | copy-start | bytes 3145732
Sparse Core Ops, SparseCore 0:
  10.7 84.7 all-gather.1
  435.0 86.5 reduce-scatter.1
